TPU v7x, 32 devices: a whole 2x2x4 slice. The times are simulated.
32 devices in a mesh: lat: 8 (over z, core), freq: 4 (over y, x).
Axes of the slice: x: 2, y: 2, z: 4, core: 2. Of those that a mesh axis runs over, the one named last changes fastest.
Arguments:
- wavefield: float32 [2, 8, 2048, 2048], P(None, 'freq', 'lat'), may hold values from -6 to 6
- source_field: float32 [2, 8, 2048, 2048], P(None, 'freq', 'lat'), may hold values from -6 to 6
- slowness: float32 [2048, 2048], P('lat', 'freq'), may hold values from 0.00015 to 0.00094
- freq_index: int32 [8], P('freq'), may hold values from 192 to 767, as said below
Outputs:
- next_field: float32 [2, 8, 2048, 2048], P(None, 'freq', 'lat')
- image: float32 [2048, 2048], P('lat', 'freq')
Inputs may be any that keep to these rules, and one draw needn't show every extreme that they name: `freq_index`: distinct frequency indices.
All inputs are finite; a program needn't handle non-finite values.
Results may differ from a plain program's by a relative error of at most 0.00013.
Values sent between devices are 32-bit elements; how exact they have to be, the bound alone decides.
A program may use at most 128 MiB of HBM per device.

v0:
```python
import math
import jax
import jax.numpy as jnp
from jax import lax
from jax.sharding import PartitionSpec as P

NX = 2048
NY = 2048
depth_step = 10.0
grid_step = 25.0
freq_step = 0.0625
highest = lax.Precision.HIGHEST
first_factor = 32


def extended(cells, sides, width):
    for axis, dim in sides:
        count = lax.axis_size(axis)
        ends = count - 1
        head = lax.slice_in_dim(cells, 0, width, axis=dim)
        tail = lax.slice_in_dim(cells, cells.shape[dim] - width, cells.shape[dim], axis=dim)
        cells = jnp.concatenate(
            [
                lax.ppermute(tail, axis, [(i, (i + 1) % count) for i in range(ends)]),
                cells,
                lax.ppermute(head, axis, [((i + 1) % count, i) for i in range(ends)]),
            ],
            axis=dim,
        )
    return cells


def fourier_tables(count):
    indices = lax.iota(jnp.int32, count)
    product = indices[:, None] * indices[None, :] % count
    angles = 2.0 * math.pi / count * product.astype(jnp.float32)
    return (jnp.cos(angles), jnp.sin(angles))


def twiddle_tables(outer, inner, count):
    left = lax.iota(jnp.int32, outer)
    right = lax.iota(jnp.int32, inner)
    product = left[:, None] * right[None, :] % count
    angles = 2.0 * math.pi / count * product.astype(jnp.float32)
    return (jnp.cos(angles), jnp.sin(angles))


def signed_waves(indices, count):
    signed = jnp.where(indices < count // 2, indices, indices - count)
    return 2.0 * math.pi / (count * grid_step) * signed.astype(jnp.float32)


def table_product(form, cos_t, sin_t, real, imag, sign):
    new_real = jnp.einsum(form, cos_t, real, precision=highest) - sign * jnp.einsum(
        form, sin_t, imag, precision=highest
    )
    new_imag = jnp.einsum(form, cos_t, imag, precision=highest) + sign * jnp.einsum(
        form, sin_t, real, precision=highest
    )
    return (new_real, new_imag)


def transform_axis(real, imag, sign, middle):
    if middle:
        members, count, other = real.shape
    else:
        members, other, count = real.shape
    inner = count // first_factor
    cos_a, sin_a = fourier_tables(first_factor)
    cos_b, sin_b = fourier_tables(inner)
    tw_cos, tw_sin = twiddle_tables(first_factor, inner, count)
    if middle:
        real = real.reshape(members, first_factor, inner, other)
        imag = imag.reshape(members, first_factor, inner, other)
        real, imag = table_product("ka,fabc->fkbc", cos_a, sin_a, real, imag, sign)
        tw_cos = tw_cos[None, :, :, None]
        tw_sin = tw_sin[None, :, :, None]
        form_two = "lb,fkbc->flkc"
    else:
        real = real.reshape(members, other, first_factor, inner)
        imag = imag.reshape(members, other, first_factor, inner)
        real, imag = table_product("ka,frab->frkb", cos_a, sin_a, real, imag, sign)
        tw_cos = tw_cos[None, None]
        tw_sin = tw_sin[None, None]
        form_two = "lb,frkb->frlk"
    turned_real = real * tw_cos - sign * imag * tw_sin
    turned_imag = imag * tw_cos + sign * real * tw_sin
    real, imag = table_product(form_two, cos_b, sin_b, turned_real, turned_imag, sign)
    if middle:
        return (real.reshape(members, count, other), imag.reshape(members, count, other))
    return (real.reshape(members, other, count), imag.reshape(members, other, count))


def spectral_step(real_part, imag_part, angular, mean_slow):
    total_y = real_part.shape[2]
    fwd_real, fwd_imag = transform_axis(real_part, imag_part, -1.0, False)
    columns = lax.all_to_all(
        jnp.stack([fwd_real, fwd_imag]), "lat", split_axis=3, concat_axis=2, tiled=True
    )
    total_x = columns.shape[2]
    spec_real, spec_imag = transform_axis(columns[0], columns[1], -1.0, True)
    width = columns.shape[3]
    col_index = lax.axis_index("lat") * width + lax.iota(jnp.int32, width)
    wave_y = signed_waves(col_index, total_y)
    wave_x = signed_waves(lax.iota(jnp.int32, total_x), total_x)
    vertical = (
        (angular * mean_slow)[:, None, None] ** 2
        - wave_x[None, :, None] ** 2
        - wave_y[None, None, :] ** 2
    )
    damping = jnp.exp(-jnp.sqrt(jnp.maximum(-vertical, 0.0)) * depth_step)
    advance = jnp.sqrt(jnp.maximum(vertical, 0.0)) * depth_step
    turn_real = damping * jnp.cos(advance)
    turn_imag = damping * jnp.sin(advance)
    shift_real = spec_real * turn_real - spec_imag * turn_imag
    shift_imag = spec_real * turn_imag + spec_imag * turn_real
    back_real, back_imag = transform_axis(shift_real, shift_imag, 1.0, True)
    back_real = back_real / total_x
    back_imag = back_imag / total_x
    strips = lax.all_to_all(
        jnp.stack([back_real, back_imag]), "lat", split_axis=2, concat_axis=3, tiled=True
    )
    out_real, out_imag = transform_axis(strips[0], strips[1], 1.0, False)
    return (out_real / total_y, out_imag / total_y)


def local(wavefield, source_field, slowness, freq_index):
    members = wavefield.shape[1]
    strip = lax.all_gather(slowness, "freq", axis=1, tiled=True)
    total = lax.psum(jnp.sum(strip), "lat")
    mean_slow = total / (NX * NY)
    angular = 2.0 * math.pi * freq_step * freq_index.astype(jnp.float32)
    lens_angle = angular[:, None, None] * (strip - mean_slow)[None] * depth_step
    lens_cos = jnp.cos(lens_angle)
    lens_sin = jnp.sin(lens_angle)
    real_part = wavefield[0] * lens_cos - wavefield[1] * lens_sin
    imag_part = wavefield[0] * lens_sin + wavefield[1] * lens_cos
    prop_real, prop_imag = spectral_step(real_part, imag_part, angular, mean_slow)
    stacked = jnp.stack([prop_real, prop_imag])
    padded = extended(stacked, (("lat", 2),), 1)
    side_pad = jnp.pad(stacked, ((0, 0), (0, 0), (0, 0), (1, 1)))
    beside_all = (
        padded[:, :, 2:, :] + padded[:, :, :-2, :] + side_pad[:, :, :, 2:] + side_pad[:, :, :, :-2]
    )
    laplace = beside_all - 4.0 * stacked
    lateral_gain = (
        depth_step
        * (
            0.5 / (angular[:, None, None] * mean_slow)
            - 0.5 / (angular[:, None, None] * strip[None])
        )
        / (grid_step * grid_step)
    )
    new_real = prop_real + lateral_gain * laplace[1]
    new_imag = prop_imag - lateral_gain * laplace[0]
    batch_total = members * lax.axis_size("freq")
    terms = jnp.sum(new_real * source_field[0] + new_imag * source_field[1], axis=0) / math.sqrt(
        batch_total
    )
    image = lax.psum_scatter(terms, "freq", scatter_dimension=1, tiled=True)
    return (jnp.stack([new_real, new_imag]), image)


def solution(mesh):
    return jax.shard_map(
        local,
        mesh=mesh,
        in_specs=(
            P(None, "freq", "lat", None),
            P(None, "freq", "lat", None),
            P("lat", "freq"),
            P("freq"),
        ),
        out_specs=(P(None, "freq", "lat", None), P("lat", "freq")),
        check_vma=False,
    )
```

profile of v0, /device:TPU:0, one launch (start us, length us, event | category | flops | bytes accessed | tf_op | source)
XLA Modules:
  0.0 928.1 jit_solution(8928447778791640208)
XLA Ops:
  9.3 8.0 fusion.360
  22.8 25.7 %all-gather.2.cloned.1.call-done = f32[256,2048]{0,1:T(8,128)} async-done(((f32[256,512]{0,1:T(8,128)}), f32[256,2048]{0,1:T(8,128)}) %all-gather.2.cloned.1.call-update) | async-done | bytes 2097168 | tf_op jit(solution)/shard_map/all_gather | solution.py:129
  56.7 17.0 %psum.7 = f32[]{:T(128)} all-reduce(f32[]{:T(128)} %reduce_sum.18), channel_id=1, replica_groups=mesh['lat'=8,'freq'=4] {'lat'}, use_global_device_ids=true, to_apply=%region_1.0 | all-reduce | flops 1 | bytes 8 | tf_op jit(solution)/shard_map/psum | solution.py:130
  77.2 17.5 %multiply_subtract_fusion.3 = (f32[2,256,32,64]{1,3,2,0:T(8,128)S(1)}, f32[2,256,32,64]{1,3,2,0:T(8,128)S(1)}) fusion(f32[2,256,32,64]{1,3,2,0:T(8,128)} %bitcast.236, f32[2,256,32,64]{1,3,2,0:T(8,128)S(1)} %bitcast.235, f32[256,32,64]{0,2,1:T(8,128)S(1)} %bitcast.243, f32[2]{0:T(128)S(1)} %get-tuple-element.34), kind=kLoop, calls=%fused_computation.85 | loop fusion | flops 8388608 | bytes 18874376 | tf_op jit(solution)/shard_map/sub | solution.py:136
  94.7 6.6 fusion.91
  101.3 7.2 fusion.89
  108.5 6.9 multiply_subtract_fusion.2
  115.4 8.3 fusion.29
  123.8 6.5 fusion.83
  130.3 7.0 fusion.81
  137.3 7.0 subtract_bitcast_fusion.1
  146.9 7.0 add_bitcast_fusion.1
  156.9 16.5 %copy.145 = f32[2,2,256,2048]{2,1,0,3:T(2,128)} copy(f32[2,2,256,2048]{2,3,1,0:T(8,128)S(1)} %pad_maximum_fusion.5) | data formatting | bytes 16777216 | tf_op jit(solution)/shard_map/stack | solution.py:98
  179.0 183.6 %all-to-all-done = f32[2,2,256,2048]{2,1,0,3:T(2,128)} async-done(((f32[2,2,256,2048]{2,1,0,3:T(2,128)}), f32[2,2,256,2048]{2,1,0,3:T(2,128)}, u32[]{:S(2)}, u32[]{:S(2)}) %all-to-all-start) | async-done | bytes 8388640 | tf_op jit(solution)/shard_map/all_to_all | solution.py:97
  377.0 10.4 %fusion.75 = f32[2,64,256,32]{2,3,1,0:T(8,128)} fusion(f32[2,32,64,256]{3,2,1,0:T(8,128)} %bitcast.229), kind=kOutput, calls=%fused_computation.131 | convolution fusion | flops 402667520 | bytes 8388608 | tf_op jit(solution)/shard_map/ka,fabc->fkbc/dot_general | solution.py:54
  387.4 7.1 fusion.73
  400.1 10.3 %multiply_subtract_fusion.1 = f32[2,64,256,32]{2,3,1,0:T(8,128)S(1)} fusion(f32[2,64,256,32]{2,3,1,0:T(8,128)} %fusion.75, f32[2,32,64,256]{3,2,1,0:T(8,128)} %bitcast.227), kind=kOutput, calls=%fused_computation.79 | convolution fusion | flops 404764672 | bytes 12582912 | tf_op jit(solution)/shard_map/ka,fabc->fkbc/dot_general | solution.py:54
  410.4 8.4 fusion.27
  418.8 6.5 fusion.67
  425.3 7.1 fusion.65
  432.4 7.0 subtract_bitcast_fusion
  441.8 7.2 add_bitcast_fusion
  451.4 19.5 %fusion.25 = (f32[2,32,64,256]{3,2,1,0:T(8,128)S(1)}, f32[2,32,64,256]{3,2,1,0:T(8,128)S(1)}) fusion(f32[256]{0:T(256)S(1)} %fusion.226, f32[2,32,64]{2,1,0:T(8,128)S(1)} %broadcast_subtract_fusion.1, f32[2,32,64,256]{3,2,1,0:T(8,128)S(1)} %bitcast.239, f32[2,32,64,256]{3,2,1,0:T(8,128)S(1)} %bitcast.237), kind=kLoop, calls=%fused_computation.53 | loop fusion | flops 15728640 | bytes 16794624 | tf_op jit(solution)/shard_map/sub | solution.py:115
  470.9 6.6 fusion.59
  477.6 7.1 fusion.57
  484.7 6.7 fusion.97
  491.4 8.4 fusion.23
  499.7 6.5 fusion.51
  506.2 6.9 fusion.49
  513.1 7.0 multiply_bitcast_fusion.3
  522.9 7.0 multiply_bitcast_fusion.2
  532.9 16.7 %copy.169 = f32[2,2,2048,256]{3,1,0,2:T(2,128)} copy(f32[2,2,2048,256]{3,2,1,0:T(8,128)S(1)} %pad_maximum_fusion.6) | data formatting | bytes 16777216 | tf_op jit(solution)/shard_map/stack | solution.py:121
  554.6 7.8 fusion.357
  573.2 165.3 %all-to-all-done.1 = f32[2,2,2048,256]{3,1,0,2:T(2,128)} async-done(((f32[2,2,2048,256]{3,1,0,2:T(2,128)}), f32[2,2,2048,256]{3,1,0,2:T(2,128)}, u32[]{:S(2)}, u32[]{:S(2)}) %all-to-all-start.1) | async-done | bytes 8388640 | tf_op jit(solution)/shard_map/all_to_all | solution.py:120
  752.8 10.4 %fusion.43 = f32[2,256,64,32]{1,3,2,0:T(8,128)} fusion(f32[2,256,32,64]{1,3,2,0:T(8,128)} %bitcast.231), kind=kOutput, calls=%fused_computation.99 | convolution fusion | flops 402667520 | bytes 8388608 | tf_op jit(solution)/shard_map/ka,frab->frkb/dot_general | solution.py:54
  763.3 7.5 fusion.41
  776.1 10.4 %fusion.103 = f32[2,256,64,32]{1,3,2,0:T(8,128)S(1)} fusion(f32[2,256,64,32]{1,3,2,0:T(8,128)} %fusion.43, f32[2,256,32,64]{1,3,2,0:T(8,128)} %bitcast.225), kind=kOutput, calls=%fused_computation.155 | convolution fusion | flops 403716096 | bytes 12582912 | tf_op jit(solution)/shard_map/ka,frab->frkb/dot_general | solution.py:54
  786.5 8.4 fusion.21
  794.9 6.4 fusion.33
  801.3 7.0 fusion.35
  808.3 7.0 multiply_bitcast_fusion
  817.8 7.3 multiply_bitcast_fusion.1
  842.2 7.4 pad_maximum_fusion
  855.1 21.9 %fusion.3 = f32[2,2,256,2048]{2,3,1,0:T(8,128)} fusion(f32[2,2,1,2048]{2,3,1,0:T(8,128)} %copy.186, f32[1,2,256,2048]{2,3,1,0:T(8,128)} %bitcast.221, f32[1,2,256,2048]{2,3,1,0:T(8,128)} %bitcast.224, f32[2,2,1,2048]{2,3,1,0:T(8,128)} %copy.184, f32[2,2,256,2048]{2,3,1,0:T(8,128)} %pad_maximum_fusion), kind=kLoop, calls=%fused_computation.9 | loop fusion | flops 18874368 | bytes 25231360 | tf_op jit(solution)/shard_map/sub | solution.py:145
  877.0 7.2 fusion.18
  885.8 7.0 multiply_add_fusion
  896.7 8.7 copy.191
  905.4 13.6 %reduce-scatter.2.cloned.1.call-done = f32[256,512]{0,1:T(8,128)} async-done(((f32[256,2048]{0,1:T(8,128)}), f32[256,512]{0,1:T(8,128)}) %reduce-scatter.2.cloned.1.call-update) | async-done | bytes 524304 | tf_op jit(solution)/shard_map/reduce_scatter | solution.py:160
  (83 shorter events, 127.6 us)
Async XLA Ops:
  7.2 41.3 %all-gather.2.cloned.1.call-start = ((), (), s32[]{:S(2)}) async-start(), calls=%async_computation.3 | async-start | bytes 2621440 | tf_op jit(solution)/shard_map/all_gather | solution.py:129
  51.2 23.8 %copy-start.16 = (s32[2]{0:T(128)S(1)}, s32[2]{0:T(128)}, u32[]{:S(2)}) copy-start(s32[2]{0:T(128)} %param.7) | copy-start | bytes 28
  51.2 24.3 %copy-start.8 = (f32[256,2048]{0,1:T(8,128)S(1)}, f32[256,2048]{0,1:T(8,128)}, u32[]{:S(2)}) copy-start(f32[256,2048]{0,1:T(8,128)} %all-gather.2.cloned.1.call-done) | copy-start | bytes 6291460
  75.0 2.2 copy-start.12
  75.5 19.2 %copy-start.13 = (f32[2]{0:T(128)}, f32[2]{0:T(128)S(1)}, u32[]{:S(2)}) copy-start(f32[2]{0:T(128)S(1)} %get-tuple-element.34) | copy-start | bytes 28
  173.4 189.3 %all-to-all-start = ((f32[2,2,256,2048]{2,1,0,3:T(2,128)}), f32[2,2,256,2048]{2,1,0,3:T(2,128)}, u32[]{:S(2)}, u32[]{:S(2)}) async-start(f32[2,2,256,2048]{2,1,0,3:T(2,128)} %copy.145), calls=%async_computation | async-start | bytes 16777216 | tf_op jit(solution)/shard_map/all_to_all | solution.py:97
  377.0 10.4 %copy-start.6 = (f32[1,2,8,256,256]{4,3,2,1,0:T(8,128)S(1)}, f32[1,2,8,256,256]{4,3,2,1,0:T(8,128)}, u32[]{:S(2)}) copy-start(f32[1,2,8,256,256]{4,3,2,1,0:T(8,128)} %copy.149) | copy-start | bytes 12582916
  400.0 10.4 %copy-start.5 = (f32[1,2,8,256,256]{4,3,2,1,0:T(8,128)S(1)}, f32[1,2,8,256,256]{4,3,2,1,0:T(8,128)}, u32[]{:S(2)}) copy-start(f32[1,2,8,256,256]{4,3,2,1,0:T(8,128)} %copy.147) | copy-start | bytes 12582916
  400.0 10.4 %copy-start.11 = (f32[2,64,256,32]{2,3,1,0:T(8,128)S(1)}, f32[2,64,256,32]{2,3,1,0:T(8,128)}, u32[]{:S(2)}) copy-start(f32[2,64,256,32]{2,3,1,0:T(8,128)} %fusion.73) | copy-start | bytes 12582916
  549.6 188.9 %all-to-all-start.1 = ((f32[2,2,2048,256]{3,1,0,2:T(2,128)}), f32[2,2,2048,256]{3,1,0,2:T(2,128)}, u32[]{:S(2)}, u32[]{:S(2)}) async-start(f32[2,2,2048,256]{3,1,0,2:T(2,128)} %copy.169), calls=%async_computation.1 | async-start | bytes 16777216 | tf_op jit(solution)/shard_map/all_to_all | solution.py:120
  554.6 364.5 %reduce-scatter.2.cloned.1.call-start = ((), (), s32[]{:S(2)}) async-start(), calls=%async_computation.4 | async-start | bytes 2621440 | tf_op jit(solution)/shard_map/reduce_scatter | solution.py:160
  752.8 10.5 %copy-start.7 = (f32[1,2,256,8,256]{2,4,3,1,0:T(8,128)S(1)}, f32[1,2,256,8,256]{2,4,3,1,0:T(8,128)}, u32[]{:S(2)}) copy-start(f32[1,2,256,8,256]{2,4,3,1,0:T(8,128)} %copy.173) | copy-start | bytes 12582916
  776.1 10.4 %copy-start.4 = (f32[1,2,256,8,256]{2,4,3,1,0:T(8,128)S(1)}, f32[1,2,256,8,256]{2,4,3,1,0:T(8,128)}, u32[]{:S(2)}) copy-start(f32[1,2,256,8,256]{2,4,3,1,0:T(8,128)} %copy.171) | copy-start | bytes 12582916
  776.1 10.4 %copy-start.10 = (f32[2,256,64,32]{1,3,2,0:T(8,128)S(1)}, f32[2,256,64,32]{1,3,2,0:T(8,128)}, u32[]{:S(2)}) copy-start(f32[2,256,64,32]{1,3,2,0:T(8,128)} %fusion.41) | copy-start | bytes 12582916
  817.8 9.8 %copy-start = (f32[2,256,64,32]{1,3,2,0:T(8,128)}, f32[2,256,64,32]{1,3,2,0:T(8,128)S(1)}, u32[]{:S(2)}) copy-start(f32[2,256,64,32]{1,3,2,0:T(8,128)S(1)} %copy.182) | copy-start | bytes 12582916
  827.6 4.6 copy-start.2
  835.0 14.6 %collective-permute-start = (f32[2,2,1,2048]{3,1,2,0:T(2,128)S(1)}, f32[2,2,1,2048]{3,1,2,0:T(2,128)S(1)}, u32[]{:S(2)}, u32[]{:S(2)}) collective-permute-start(f32[2,2,1,2048]{3,1,2,0:T(2,128)S(1)} %copy.183), channel_id=1, source_target_pairs={{4,0},{8,4},{12,8},{16,12},{20,16},{24,20},{28,24},{5,1},{9,5},{13... | collective-permute-start | bytes 98312 | tf_op jit(solution)/shard_map/ppermute | solution.py:26
  839.2 13.2 %collective-permute-start.1 = (f32[2,2,1,2048]{3,1,2,0:T(2,128)S(1)}, f32[2,2,1,2048]{3,1,2,0:T(2,128)S(1)}, u32[]{:S(2)}, u32[]{:S(2)}) collective-permute-start(f32[2,2,1,2048]{3,1,2,0:T(2,128)S(1)} %copy.185), channel_id=1, source_target_pairs={{0,4},{4,8},{8,12},{12,16},{16,20},{20,24},{24,28},{1,5},{5,9},{9,... | collective-permute-start | bytes 98312 | tf_op jit(solution)/shard_map/ppermute | solution.py:24
  855.0 21.9 %copy-start.1 = (f32[2,256,64,32]{1,3,2,0:T(8,128)S(1)}, f32[2,256,64,32]{1,3,2,0:T(8,128)}, u32[]{:S(2)}) copy-start(f32[2,256,64,32]{1,3,2,0:T(8,128)} %copy-done) | copy-start | bytes 12582916
  855.1 21.9 %copy-start.3 = (f32[2,256,64,32]{1,3,2,0:T(8,128)S(1)}, f32[2,256,64,32]{1,3,2,0:T(8,128)}, u32[]{:S(2)}) copy-start(f32[2,256,64,32]{1,3,2,0:T(8,128)} %copy-done.2) | copy-start | bytes 12582916
  855.1 21.9 %copy-start.9 = (f32[256,2048]{0,1:T(8,128)S(1)}, f32[256,2048]{0,1:T(8,128)}, u32[]{:S(2)}) copy-start(f32[256,2048]{0,1:T(8,128)} %all-gather.2.cloned.1.call-done) | copy-start | bytes 6291460
  855.1 21.9 %copy-start.14 = (f32[2]{0:T(128)S(1)}, f32[2]{0:T(128)}, u32[]{:S(2)}) copy-start(f32[2]{0:T(128)} %copy-done.13) | copy-start | bytes 28
  855.1 21.9 %copy-start.15 = (f32[2]{0:T(128)S(1)}, f32[2]{0:T(128)}, u32[]{:S(2)}) copy-start(f32[2]{0:T(128)} %get-tuple-element.32) | copy-start | bytes 28
Sparse Core Ops, SparseCore 0:
  10.4 38.0 all-gather.1
  885.9 33.0 reduce-scatter.1
where the time goes:
time: 933 us; the launch traced here: 928 us
  waiting for transfers between devices  388 us (42%)
  matrix products  241 us (26%)
  local copies, waits for them, and re-layouts  156 us (17%)
  other arithmetic  95.3 us (10%)
  blocking collectives  17 us (2%)
  between operations  16.1 us (2%)
  starting transfers between devices  14.7 us (2%)
    all_to_all x1, waiting for transfers between devices, spectral_step(): lax.all_to_all(jnp.stack([fwd_real, fwd_imag]), 'lat', split_axis=3, conc...  184 us
    all_to_all x1, waiting for transfers between devices, spectral_step(): lax.all_to_all(jnp.stack([back_real, back_imag]), 'lat', split_axis=2, co...  165 us
    dot_general x8, matrix products, table_product(): jnp.einsum(form, cos_t, real, precision=highest)  62.6 us
    dot_general x8, matrix products, table_product(): jnp.einsum(form, sin_t, real, precision=highest)  61.6 us
    dot_general x8, matrix products, table_product(): jnp.einsum(form, sin_t, imag, precision=highest)  60.6 us
    dot_general x8, matrix products, table_product(): jnp.einsum(form, cos_t, imag, precision=highest)  56.2 us
    unnamed x41, local copies, waits for them, and re-layouts  36.1 us
    all_gather x1, waiting for transfers between devices, local(): strip = lax.all_gather(slowness, 'freq', axis=1, tiled=True)  25.7 us
  transfers between devices with their start and end apart: 6, of which 4 were waited for; matrix products, arithmetic and copies ran while one was open for 7% of the time, Pallas kernels for 0%

commit v1 on v0

--- a/solution.py
+++ b/solution.py
@@ -11,6 +11,29 @@
 freq_step = 0.0625
 highest = lax.Precision.HIGHEST
 first_factor = 32
+
+
+def cut_along(array, dim, count):
+    dims = array.shape
+    pieces = array.reshape(*dims[:dim], count, dims[dim] // count, *dims[dim + 1 :])
+    return jnp.moveaxis(pieces, dim, 0)
+
+
+def in_order(blocks, dim):
+    shape = list(blocks.shape[1:])
+    shape[dim] *= blocks.shape[0]
+    return jnp.moveaxis(blocks, 0, dim).reshape(shape)
+
+
+def exchange_in_pairs(array, axis, split_dim, concat_dim):
+    length, index = (lax.axis_size(axis), lax.axis_index(axis))
+    parts = cut_along(array, split_dim, length)
+    done = [parts[index]]
+    for hop in range(1, length):
+        sent = parts[index ^ hop]
+        done.append(lax.ppermute(sent, axis, [(i, i ^ hop) for i in range(length)]))
+    parts = jnp.stack(done)[index ^ jnp.arange(length)]
+    return in_order(parts, concat_dim)
 
 
 def extended(cells, sides, width):
@@ -94,9 +117,7 @@
 def spectral_step(real_part, imag_part, angular, mean_slow):
     total_y = real_part.shape[2]
     fwd_real, fwd_imag = transform_axis(real_part, imag_part, -1.0, False)
-    columns = lax.all_to_all(
-        jnp.stack([fwd_real, fwd_imag]), "lat", split_axis=3, concat_axis=2, tiled=True
-    )
+    columns = exchange_in_pairs(jnp.stack([fwd_real, fwd_imag]), "lat", 3, 2)
     total_x = columns.shape[2]
     spec_real, spec_imag = transform_axis(columns[0], columns[1], -1.0, True)
     width = columns.shape[3]

time: 933 us -> 902 us (0.967)
  waiting for transfers between devices: 388 us -> 318 us
  starting transfers between devices: 14.7 us -> 49.8 us
    all_to_all x1 -> x0, waiting for transfers between devices: 184 us -> none  [spectral_step(): lax.all_to_all(jnp.stack([fwd_real, fwd_imag]), 'lat', split_axis=3, conc...]
    ppermute x0 -> x7, waiting for transfers between devices: none -> 118 us  [exchange_in_pairs(): done.append(lax.ppermute(sent, axis, [(i, i ^ hop) for i in range(length)]))]
    all_to_all x1, starting transfers between devices: 4.96 us -> 40.1 us  [spectral_step(): lax.all_to_all(jnp.stack([back_real, back_imag]), 'lat', split_axis=2, co...]
    unnamed x41 -> x44, local copies, waits for them, and re-layouts: 36.1 us -> 48.9 us
    slice x3, local copies, waits for them, and re-layouts: 14.9 us -> 5.18 us  [spectral_step(): spec_real, spec_imag = transform_axis(columns[0], columns[1], -1.0, True)]
  transfers between devices with their start and end apart: 6 -> 12, of which waited for: 4 -> 6; matrix products, arithmetic and copies ran while one was open for 7% -> 11% of each run, Pallas kernels for 0% -> 0%
where the time goes in v1:
time: 902 us; the launch traced here: 897 us
  waiting for transfers between devices  318 us (35%)
  matrix products  234 us (26%)
  local copies, waits for them, and re-layouts  160 us (18%)
  other arithmetic  101 us (11%)
  starting transfers between devices  49.8 us (6%)
  blocking collectives  17 us (2%)
  between operations  16.1 us (2%)
    all_to_all x1, waiting for transfers between devices, spectral_step(): lax.all_to_all(jnp.stack([back_real, back_imag]), 'lat', split_axis=2, co...  166 us
    ppermute x7, waiting for transfers between devices, exchange_in_pairs(): done.append(lax.ppermute(sent, axis, [(i, i ^ hop) for i in range(length)]))  118 us
    dot_general x8, matrix products, table_product(): jnp.einsum(form, sin_t, real, precision=highest)  61.9 us
    dot_general x8, matrix products, table_product(): jnp.einsum(form, cos_t, real, precision=highest)  59.6 us
    dot_general x8, matrix products, table_product(): jnp.einsum(form, sin_t, imag, precision=highest)  57.2 us
    dot_general x8, matrix products, table_product(): jnp.einsum(form, cos_t, imag, precision=highest)  55.2 us
    unnamed x44, local copies, waits for them, and re-layouts  48.9 us
    all_to_all x1, starting transfers between devices, spectral_step(): lax.all_to_all(jnp.stack([back_real, back_imag]), 'lat', split_axis=2, co...  40.1 us
  transfers between devices with their start and end apart: 12, of which 6 were waited for; matrix products, arithmetic and copies ran while one was open for 11% of the time, Pallas kernels for 0%

profile of v1, /device:TPU:0, one launch (start us, length us, event | category | flops | bytes accessed | tf_op | source)
XLA Modules:
  0.0 896.6 jit_solution(8383530016802950509)
XLA Ops:
  9.3 8.0 fusion.369
  28.3 20.2 %all-gather.2.cloned.1.call-done = f32[256,2048]{0,1:T(8,128)} async-done(((f32[256,512]{0,1:T(8,128)}), f32[256,2048]{0,1:T(8,128)}) %all-gather.2.cloned.1.call-update) | async-done | bytes 2097168 | tf_op jit(solution)/shard_map/all_gather | solution.py:150
  51.2 17.0 %psum.7 = f32[]{:T(128)} all-reduce(f32[]{:T(128)} %reduce_sum.18), channel_id=1, replica_groups=mesh['lat'=8,'freq'=4] {'lat'}, use_global_device_ids=true, to_apply=%region_1.0 | all-reduce | flops 1 | bytes 8 | tf_op jit(solution)/shard_map/psum | solution.py:151
  72.3 17.5 %multiply_subtract_fusion.3 = (f32[2,256,32,64]{1,3,2,0:T(8,128)S(1)}, f32[2,256,32,64]{1,3,2,0:T(8,128)S(1)}) fusion(f32[2,256,32,64]{1,3,2,0:T(8,128)} %bitcast.263, f32[2,256,32,64]{1,3,2,0:T(8,128)S(1)} %bitcast.262, f32[256,32,64]{0,2,1:T(8,128)S(1)} %bitcast.268, f32[2]{0:T(128)S(1)} %get-tuple-element.44), kind=kLoop, calls=%fused_computation.101 | loop fusion | flops 8388608 | bytes 18874376 | tf_op jit(solution)/shard_map/sub | solution.py:157
  96.5 7.2 fusion.89
  103.6 6.9 multiply_subtract_fusion.2
  110.5 8.3 fusion.29
  118.9 6.7 fusion.81
  125.6 6.7 fusion.83
  132.3 7.2 add_bitcast_fusion.1
  142.3 7.0 subtract_bitcast_fusion.1
  179.4 21.0 %collective-permute-done.1 = f32[2,2,256,256]{3,2,1,0:T(8,128)} collective-permute-done((f32[2,2,256,256]{3,2,1,0:T(8,128)}, f32[2,2,256,256]{3,2,1,0:T(8,128)}, u32[]{:S(2)}, u32[]{:S(2)}) %collective-permute-start.1) | collective-permute-done | bytes 1048608 | tf_op jit(solution)/shard_map/ppermute | solution.py:34
  203.3 41.2 %collective-permute-done.2 = f32[2,2,256,256]{3,2,1,0:T(8,128)} collective-permute-done((f32[2,2,256,256]{3,2,1,0:T(8,128)}, f32[2,2,256,256]{3,2,1,0:T(8,128)}, u32[]{:S(2)}, u32[]{:S(2)}) %collective-permute-start.2) | collective-permute-done | bytes 1048608 | tf_op jit(solution)/shard_map/ppermute | solution.py:34
  246.8 55.8 %collective-permute-done.3 = f32[2,2,256,256]{3,2,1,0:T(8,128)} collective-permute-done((f32[2,2,256,256]{3,2,1,0:T(8,128)}, f32[2,2,256,256]{3,2,1,0:T(8,128)}, u32[]{:S(2)}, u32[]{:S(2)}) %collective-permute-start.3) | collective-permute-done | bytes 1048608 | tf_op jit(solution)/shard_map/ppermute | solution.py:34
  309.2 7.7 gather_fusion
  321.8 6.6 fusion.75
  328.5 6.9 fusion.73
  335.7 6.9 multiply_subtract_fusion.1
  342.6 8.5 fusion.27
  351.2 6.7 fusion.67
  357.9 6.7 fusion.65
  364.5 7.4 subtract_bitcast_fusion
  374.4 7.0 add_bitcast_fusion
  384.0 19.3 %fusion.25 = (f32[2,32,64,256]{3,2,1,0:T(8,128)S(1)}, f32[2,32,64,256]{3,2,1,0:T(8,128)S(1)}) fusion(f32[256]{0:T(256)S(1)} %fusion.266, f32[2,32,64]{2,1,0:T(8,128)S(1)} %broadcast_subtract_fusion.1, f32[2,32,64,256]{3,2,1,0:T(8,128)S(1)} %bitcast.265, f32[2,32,64,256]{3,2,1,0:T(8,128)S(1)} %bitcast.264), kind=kLoop, calls=%fused_computation.69 | loop fusion | flops 15728640 | bytes 16794624 | tf_op jit(solution)/shard_map/sub | solution.py:136
  403.3 6.6 fusion.59
  410.0 7.1 fusion.57
  417.0 6.7 fusion.97
  423.7 8.4 fusion.23
  438.6 6.9 fusion.49
  445.5 7.0 multiply_bitcast_fusion.3
  455.3 7.0 multiply_bitcast_fusion.2
  465.3 16.7 %copy.242 = f32[2,2,2048,256]{3,1,0,2:T(2,128)} copy(f32[2,2,2048,256]{3,2,1,0:T(8,128)S(1)} %pad_maximum_fusion.5) | data formatting | bytes 16777216 | tf_op jit(solution)/shard_map/stack | solution.py:142
  482.0 40.1 %all-to-all-start = ((f32[2,2,2048,256]{3,1,0,2:T(2,128)}), f32[2,2,2048,256]{3,1,0,2:T(2,128)}, u32[]{:S(2)}, u32[]{:S(2)}) async-start(f32[2,2,2048,256]{3,1,0,2:T(2,128)} %copy.242), calls=%async_computation | async-start | bytes 16777216 | tf_op jit(solution)/shard_map/all_to_all | solution.py:141
  522.1 7.8 fusion.366
  540.7 166.2 %all-to-all-done = f32[2,2,2048,256]{3,1,0,2:T(2,128)} async-done(((f32[2,2,2048,256]{3,1,0,2:T(2,128)}), f32[2,2,2048,256]{3,1,0,2:T(2,128)}, u32[]{:S(2)}, u32[]{:S(2)}) %all-to-all-start) | async-done | bytes 8388640 | tf_op jit(solution)/shard_map/all_to_all | solution.py:141
  721.2 10.4 %fusion.43 = f32[2,256,64,32]{1,3,2,0:T(8,128)} fusion(f32[2,256,32,64]{1,3,2,0:T(8,128)} %bitcast.254), kind=kOutput, calls=%fused_computation.115 | convolution fusion | flops 402667520 | bytes 8388608 | tf_op jit(solution)/shard_map/ka,frab->frkb/dot_general | solution.py:77
  731.6 7.4 fusion.41
  744.4 10.4 %fusion.103 = f32[2,256,64,32]{1,3,2,0:T(8,128)S(1)} fusion(f32[2,256,64,32]{1,3,2,0:T(8,128)} %fusion.43, f32[2,256,32,64]{1,3,2,0:T(8,128)} %bitcast.248), kind=kOutput, calls=%fused_computation.171 | convolution fusion | flops 403716096 | bytes 12582912 | tf_op jit(solution)/shard_map/ka,frab->frkb/dot_general | solution.py:77
  754.9 8.4 fusion.21
  769.7 7.0 fusion.35
  776.7 7.0 multiply_bitcast_fusion
  786.2 7.3 multiply_bitcast_fusion.1
  810.6 7.4 pad_maximum_fusion
  823.5 21.9 %fusion.3 = f32[2,2,256,2048]{2,3,1,0:T(8,128)} fusion(f32[2,2,1,2048]{2,3,1,0:T(8,128)} %copy.259, f32[1,2,256,2048]{2,3,1,0:T(8,128)} %bitcast.244, f32[1,2,256,2048]{2,3,1,0:T(8,128)} %bitcast.247, f32[2,2,1,2048]{2,3,1,0:T(8,128)} %copy.257, f32[2,2,256,2048]{2,3,1,0:T(8,128)} %pad_maximum_fusion), kind=kLoop, calls=%fused_computation.26 | loop fusion | flops 18874368 | bytes 25231360 | tf_op jit(solution)/shard_map/sub | solution.py:166
  845.4 7.2 fusion.18
  854.2 7.0 multiply_add_fusion
  865.1 8.7 copy.264
  873.8 13.7 %reduce-scatter.2.cloned.1.call-done = f32[256,512]{0,1:T(8,128)} async-done(((f32[256,2048]{0,1:T(8,128)}), f32[256,512]{0,1:T(8,128)}) %reduce-scatter.2.cloned.1.call-update) | async-done | bytes 524304 | tf_op jit(solution)/shard_map/reduce_scatter | solution.py:181
  (109 shorter events, 161.9 us)
Async XLA Ops:
  7.2 41.3 %all-gather.2.cloned.1.call-start = ((), (), s32[]{:S(2)}) async-start(), calls=%async_computation.2 | async-start | bytes 2621440 | tf_op jit(solution)/shard_map/all_gather | solution.py:150
  22.7 46.7 %copy-start.14 = (s32[2]{0:T(128)S(1)}, s32[2]{0:T(128)}, u32[]{:S(2)}) copy-start(s32[2]{0:T(128)} %param.7) | copy-start | bytes 28
  69.5 2.8 copy-start.10
  70.0 19.8 %copy-start.11 = (f32[2]{0:T(128)}, f32[2]{0:T(128)S(1)}, u32[]{:S(2)}) copy-start(f32[2]{0:T(128)S(1)} %get-tuple-element.44) | copy-start | bytes 28
  142.3 9.5 %copy-start.6 = (f32[2,256,64,32]{1,3,2,0:T(8,128)}, f32[2,256,64,32]{1,3,2,0:T(8,128)S(1)}, u32[]{:S(2)}) copy-start(f32[2,256,64,32]{1,3,2,0:T(8,128)S(1)} %copy.211) | copy-start | bytes 12582916
  151.8 3.0 copy-start.7
  157.3 19.8 %collective-permute-start = (f32[2,2,256,256]{3,2,1,0:T(8,128)}, f32[2,2,256,256]{3,2,1,0:T(8,128)}, u32[]{:S(2)}, u32[]{:S(2)}) collective-permute-start(f32[2,2,256,256]{3,2,1,0:T(8,128)} %bitcast.269), channel_id=1, source_target_pairs={{0,4},{4,0},{8,12},{12,8},{16,20},{20,16},{24,28},{28,24},{1,5},{5... | collective-permute-start | bytes 3145736 | tf_op jit(solution)/shard_map/ppermute | solution.py:34
  158.8 41.6 %collective-permute-start.1 = (f32[2,2,256,256]{3,2,1,0:T(8,128)}, f32[2,2,256,256]{3,2,1,0:T(8,128)}, u32[]{:S(2)}, u32[]{:S(2)}) collective-permute-start(f32[2,2,256,256]{3,2,1,0:T(8,128)} %bitcast.271), channel_id=1, source_target_pairs={{0,8},{4,12},{8,0},{12,4},{16,24},{20,28},{24,16},{28,20},{1,9},{5... | collective-permute-start | bytes 3145736 | tf_op jit(solution)/shard_map/ppermute | solution.py:34
  162.8 142.0 %collective-permute-start.4 = (f32[2,2,256,256]{3,2,1,0:T(8,128)}, f32[2,2,256,256]{3,2,1,0:T(8,128)}, u32[]{:S(2)}, u32[]{:S(2)}) collective-permute-start(f32[2,2,256,256]{3,2,1,0:T(8,128)} %bitcast.270), channel_id=1, source_target_pairs={{0,20},{4,16},{8,28},{12,24},{16,4},{20,0},{24,12},{28,8},{1,21},{... | collective-permute-start | bytes 3145736 | tf_op jit(solution)/shard_map/ppermute | solution.py:34
  167.1 77.4 %collective-permute-start.2 = (f32[2,2,256,256]{3,2,1,0:T(8,128)}, f32[2,2,256,256]{3,2,1,0:T(8,128)}, u32[]{:S(2)}, u32[]{:S(2)}) collective-permute-start(f32[2,2,256,256]{3,2,1,0:T(8,128)} %bitcast.275), channel_id=1, source_target_pairs={{0,12},{4,8},{8,4},{12,0},{16,28},{20,24},{24,20},{28,16},{1,13},{... | collective-permute-start | bytes 3145736 | tf_op jit(solution)/shard_map/ppermute | solution.py:34
  170.3 132.3 %collective-permute-start.3 = (f32[2,2,256,256]{3,2,1,0:T(8,128)}, f32[2,2,256,256]{3,2,1,0:T(8,128)}, u32[]{:S(2)}, u32[]{:S(2)}) collective-permute-start(f32[2,2,256,256]{3,2,1,0:T(8,128)} %bitcast.274), channel_id=1, source_target_pairs={{0,16},{4,20},{8,24},{12,28},{16,0},{20,4},{24,8},{28,12},{1,17},{... | collective-permute-start | bytes 3145736 | tf_op jit(solution)/shard_map/ppermute | solution.py:34
  177.1 130.1 %collective-permute-start.5 = (f32[2,2,256,256]{3,2,1,0:T(8,128)}, f32[2,2,256,256]{3,2,1,0:T(8,128)S(1)}, u32[]{:S(2)}, u32[]{:S(2)}) collective-permute-start(f32[2,2,256,256]{3,2,1,0:T(8,128)} %bitcast.273), channel_id=1, source_target_pairs={{0,24},{4,28},{8,16},{12,20},{16,8},{20,12},{24,0},{28,4},{1,25},{... | collective-permute-start | bytes 3145736 | tf_op jit(solution)/shard_map/ppermute | solution.py:34
  200.4 107.8 %collective-permute-start.6 = (f32[2,2,256,256]{3,2,1,0:T(8,128)S(1)}, f32[2,2,256,256]{3,2,1,0:T(8,128)S(1)}, u32[]{:S(2)}, u32[]{:S(2)}) collective-permute-start(f32[2,2,256,256]{3,2,1,0:T(8,128)S(1)} %bitcast.272), channel_id=1, source_target_pairs={{0,28},{4,24},{8,20},{12,16},{16,12},{20,8},{24,4},{28,0},{1,29},{... | collective-permute-start | bytes 3145736 | tf_op jit(solution)/shard_map/ppermute | solution.py:34
  482.0 224.9 %all-to-all-start = ((f32[2,2,2048,256]{3,1,0,2:T(2,128)}), f32[2,2,2048,256]{3,1,0,2:T(2,128)}, u32[]{:S(2)}, u32[]{:S(2)}) async-start(f32[2,2,2048,256]{3,1,0,2:T(2,128)} %copy.242), calls=%async_computation | async-start | bytes 16777216 | tf_op jit(solution)/shard_map/all_to_all | solution.py:141
  522.1 365.5 %reduce-scatter.2.cloned.1.call-start = ((), (), s32[]{:S(2)}) async-start(), calls=%async_computation.3 | async-start | bytes 2621440 | tf_op jit(solution)/shard_map/reduce_scatter | solution.py:181
  721.2 10.4 %copy-start.5 = (f32[1,2,256,8,256]{2,4,3,1,0:T(8,128)S(1)}, f32[1,2,256,8,256]{2,4,3,1,0:T(8,128)}, u32[]{:S(2)}) copy-start(f32[1,2,256,8,256]{2,4,3,1,0:T(8,128)} %copy.246) | copy-start | bytes 12582916
  744.4 10.4 %copy-start.4 = (f32[1,2,256,8,256]{2,4,3,1,0:T(8,128)S(1)}, f32[1,2,256,8,256]{2,4,3,1,0:T(8,128)}, u32[]{:S(2)}) copy-start(f32[1,2,256,8,256]{2,4,3,1,0:T(8,128)} %copy.244) | copy-start | bytes 12582916
  744.4 10.4 %copy-start.9 = (f32[2,256,64,32]{1,3,2,0:T(8,128)S(1)}, f32[2,256,64,32]{1,3,2,0:T(8,128)}, u32[]{:S(2)}) copy-start(f32[2,256,64,32]{1,3,2,0:T(8,128)} %fusion.41) | copy-start | bytes 12582916
  786.2 9.8 %copy-start = (f32[2,256,64,32]{1,3,2,0:T(8,128)}, f32[2,256,64,32]{1,3,2,0:T(8,128)S(1)}, u32[]{:S(2)}) copy-start(f32[2,256,64,32]{1,3,2,0:T(8,128)S(1)} %copy.255) | copy-start | bytes 12582916
  796.0 4.6 copy-start.2
  803.4 14.6 %collective-permute-start.7 = (f32[2,2,1,2048]{3,1,2,0:T(2,128)S(1)}, f32[2,2,1,2048]{3,1,2,0:T(2,128)S(1)}, u32[]{:S(2)}, u32[]{:S(2)}) collective-permute-start(f32[2,2,1,2048]{3,1,2,0:T(2,128)S(1)} %copy.256), channel_id=1, source_target_pairs={{4,0},{8,4},{12,8},{16,12},{20,16},{24,20},{28,24},{5,1},{9,5},{13... | collective-permute-start | bytes 98312 | tf_op jit(solution)/shard_map/ppermute | solution.py:49
  807.5 13.2 %collective-permute-start.8 = (f32[2,2,1,2048]{3,1,2,0:T(2,128)S(1)}, f32[2,2,1,2048]{3,1,2,0:T(2,128)S(1)}, u32[]{:S(2)}, u32[]{:S(2)}) collective-permute-start(f32[2,2,1,2048]{3,1,2,0:T(2,128)S(1)} %copy.258), channel_id=1, source_target_pairs={{0,4},{4,8},{8,12},{12,16},{16,20},{20,24},{24,28},{1,5},{5,9},{9,... | collective-permute-start | bytes 98312 | tf_op jit(solution)/shard_map/ppermute | solution.py:47
  823.4 21.9 %copy-start.1 = (f32[2,256,64,32]{1,3,2,0:T(8,128)S(1)}, f32[2,256,64,32]{1,3,2,0:T(8,128)}, u32[]{:S(2)}) copy-start(f32[2,256,64,32]{1,3,2,0:T(8,128)} %copy-done) | copy-start | bytes 12582916
  823.4 21.9 %copy-start.3 = (f32[2,256,64,32]{1,3,2,0:T(8,128)S(1)}, f32[2,256,64,32]{1,3,2,0:T(8,128)}, u32[]{:S(2)}) copy-start(f32[2,256,64,32]{1,3,2,0:T(8,128)} %copy-done.2) | copy-start | bytes 12582916
  823.4 21.9 %copy-start.8 = (f32[256,2048]{0,1:T(8,128)S(1)}, f32[256,2048]{0,1:T(8,128)}, u32[]{:S(2)}) copy-start(f32[256,2048]{0,1:T(8,128)} %all-gather.2.cloned.1.call-done) | copy-start | bytes 6291460
  823.4 21.9 %copy-start.12 = (f32[2]{0:T(128)S(1)}, f32[2]{0:T(128)}, u32[]{:S(2)}) copy-start(f32[2]{0:T(128)} %copy-done.11) | copy-start | bytes 28
  823.4 21.9 %copy-start.13 = (f32[2]{0:T(128)S(1)}, f32[2]{0:T(128)}, u32[]{:S(2)}) copy-start(f32[2]{0:T(128)} %get-tuple-element.42) | copy-start | bytes 28
Sparse Core Ops, SparseCore 0:
  10.4 38.0 all-gather.1
  854.3 33.1 reduce-scatter.1
